TPU v7x, 32 devices: a whole 2x2x4 slice. The times are simulated.
32 devices in a mesh: groups: 2 (over x), row: 16 (over z, y, core).
Axes of the slice: x: 2, y: 2, z: 4, core: 2. Of those that a mesh axis runs over, the one named last changes fastest.
Arguments:
- base_grid: float32 [8192, 2048], P(('groups', 'row')), parts along dimension 0, may hold values from -6 to 6
- strip_minima: float32 [4096, 8, 128], P(('groups', 'row')), parts along dimension 0, may hold values from -6 to 6
- strip_owner: int32 [4096, 1], P(('groups', 'row')), parts along dimension 0, may hold values from 0 to 15; in each aligned block of 128 rows (0 to 127, 128 to 255, ...) at most 16 rows name the same one
- strip_cell: int32 [4096], P(('groups', 'row')), parts along dimension 0, may hold values from 0 to 511
Outputs:
- merged: float32 [8192, 2048], P(('groups', 'row')), parts along dimension 0
- opened_first: float32 [8192, 2048], P(('groups', 'row')), parts along dimension 0
- ground: float32 [8192, 2048], P(('groups', 'row')), parts along dimension 0
There are 2 independent parts, one for each index of `groups`. A program takes and returns all parts, laid end to end along the dimension named above; each array names one. Nothing has to cross between parts.
Inputs may be any that keep to these rules, and one draw needn't show every extreme that they name: `strip_owner`: among the strip blocks of one device no owner is named more than 16 times, a bound that some block reaches.
All inputs are finite; a program needn't handle non-finite values.
Results may differ from a plain program's by a relative error of at most 0.00002.
Values sent between devices are 32-bit elements; how exact they have to be, the bound alone decides.
A program may use at most 64 MiB of HBM per device.

v0:
```python
import functools

import jax
import jax.numpy as jnp
from jax import lax
from jax.experimental import pallas as pl
from jax.experimental.pallas import tpu as pltpu
from jax.sharding import PartitionSpec as P

BR = 8
BC = 128
HALF1 = 32
HALF2 = 64
TALL = 64
PIECES = 4
MESH = pl.DeviceIdType.MESH
VMEM_LIMIT = 48 * 1024 * 1024


def pack_kernel(count, capacity, held, owner_ref, cell_ref, strips_ref, box_ref, used_ref):
    lane = lax.broadcasted_iota(jnp.int32, (1, BC), 1)

    def clear(i, c):
        used_ref[i] = 0
        box_ref[i, capacity] = jnp.full((BR, BC), -1.0, jnp.float32)
        return c

    lax.fori_loop(0, count, clear, 0)

    def place(k, c):
        owner = owner_ref[k]
        slot = used_ref[owner]
        used_ref[owner] = slot + 1
        box_ref[owner, slot] = strips_ref[k]
        tags = box_ref[owner, capacity, 0:1, :]
        box_ref[owner, capacity, 0:1, :] = jnp.where(
            lane == slot, cell_ref[k].astype(jnp.float32), tags
        )
        return c

    lax.fori_loop(0, held, place, 0)


def exchange_kernel(n, box_ref, grid_ref, in_ref, base_ref, send_sem, recv_sem, own_sem, base_sem):
    me = lax.axis_index("row")
    barrier = pltpu.get_barrier_semaphore()

    def greet(k, c):
        peer = lax.rem(me + k, n)
        pl.semaphore_signal(barrier, inc=1, device_id={"row": peer}, device_id_type=MESH)
        return c

    lax.fori_loop(1, n, greet, 0)
    own = pltpu.make_async_copy(box_ref.at[me], in_ref.at[me], own_sem)
    own.start()
    base = pltpu.make_async_copy(grid_ref, base_ref, base_sem)
    base.start()
    pl.semaphore_wait(barrier, n - 1)

    def copy(peer, slot):
        return pltpu.make_async_remote_copy(
            src_ref=box_ref.at[peer],
            dst_ref=in_ref.at[slot],
            send_sem=send_sem.at[peer],
            recv_sem=recv_sem.at[slot],
            device_id={"row": peer},
            device_id_type=MESH,
        )

    def send(k, c):
        copy(lax.rem(me + k, n), me).start()
        return c

    lax.fori_loop(1, n, send, 0)

    def finish(k, c):
        peer = lax.rem(me + k, n)
        copy(peer, peer).wait_recv()
        copy(peer, me).wait_send()
        return c

    lax.fori_loop(1, n, finish, 0)
    own.wait()
    base.wait()


def merge_kernel(n, capacity, col_blocks, tags_ref, base_ref, box_ref, out_ref):
    out_ref[...] = base_ref[...]
    bits = col_blocks.bit_length() - 1

    def place(s, c):
        for j in range(capacity):
            tag = tags_ref[s * capacity + j]
            cell = jnp.maximum(tag, 0)
            row = pl.multiple_of((cell >> bits) * BR, BR)
            col = pl.multiple_of((cell & (col_blocks - 1)) * BC, BC)
            here = (pl.ds(row, BR), pl.ds(col, BC))
            block = jnp.where(tag >= 0, box_ref[s, j], jnp.inf)
            out_ref[here] = jnp.minimum(out_ref[here], block)
        return c

    lax.fori_loop(0, n, place, 0)


def across(x, half, take_min):
    combine = jnp.minimum if take_min else jnp.maximum
    fill = jnp.inf if take_min else -jnp.inf
    cols = x.shape[1]
    run = jnp.concatenate([x, jnp.full((x.shape[0], BC), fill, jnp.float32)], axis=1)
    width = cols + BC
    span = 1
    while span < half:
        run = combine(run, pltpu.roll(run, width - span, axis=1))
        span *= 2
    run = combine(run, pltpu.roll(run, half, axis=1))
    run = combine(run, pltpu.roll(run, width - 1, axis=1))
    return run[:, :cols]


def down(x, half, take_min):
    combine = jnp.minimum if take_min else jnp.maximum
    rows = x.shape[0]
    run = x
    span = 1
    while span < 8:
        run = combine(run, pltpu.roll(run, rows - span, axis=0))
        span *= 2
    while span < 2 * half:
        size = run.shape[0]
        run = combine(run[: size - span], run[span:])
        span *= 2
    keep = rows - 2 * half
    return combine(run[:keep], x[2 * half :])


def open_rows(src, first, out, dst, dst_first, half, is_top, is_bottom, start=0, stop=None):
    def body(c, carry):
        cols = pl.ds(pl.multiple_of(c * BC, BC), BC)
        low = down(src[first : first + out + 4 * half, cols], half, True)
        parts = [low[:half], low[half : half + out], low[half + out :]]
        if is_top is not None:
            parts[0] = jnp.where(is_top, -jnp.inf, parts[0])
        if is_bottom is not None:
            parts[2] = jnp.where(is_bottom, -jnp.inf, parts[2])
        dst[dst_first : dst_first + out, cols] = down(jnp.concatenate(parts, axis=0), half, False)
        return carry

    lax.fori_loop(start, src.shape[1] // BC if stop is None else stop, body, 0)


def row_blocks(first, rows, body):
    def step(i, c):
        body(pl.multiple_of(first + i * TALL, TALL))
        return c

    lax.fori_loop(0, rows // TALL, step, 0)


def open_kernel(n, m_ref, first_ref, ground_ref, near, far, mid, send_sem, recv_sem):
    place = lax.axis_index("row")
    rows = m_ref.shape[0]
    is_top, is_bottom = place == 0, place == n - 1
    edge1, edge2 = 2 * HALF1, 2 * HALF2
    width = m_ref.shape[1] // PIECES

    barrier = pltpu.get_barrier_semaphore()

    @pl.when(place > 0)
    def _():
        pl.semaphore_signal(barrier, inc=1, device_id={"row": place - 1}, device_id_type=MESH)

    @pl.when(place < n - 1)
    def _():
        pl.semaphore_signal(barrier, inc=1, device_id={"row": place + 1}, device_id_type=MESH)

    pl.semaphore_wait(barrier, jnp.where(is_top | is_bottom, 1, 2))

    def move(buf, src, dst, size, cols, peer, at):
        return pltpu.make_async_remote_copy(
            src_ref=buf.at[pl.ds(src, size), cols],
            dst_ref=buf.at[pl.ds(dst, size), cols],
            send_sem=send_sem.at[at],
            recv_sem=recv_sem.at[at],
            device_id={"row": peer},
            device_id_type=MESH,
        )

    plans = [
        (near, (edge1, edge1 + rows, edge1), (rows, 0, edge1), pl.ds(0, m_ref.shape[1])),
        (far, (edge2 + 64, edge2 + rows + 64, 64), (edge2 + 128, 0, 64), pl.ds(0, m_ref.shape[1])),
    ] + [
        (far, (edge2, edge2 + rows, 64), (edge2 + 192, 64, 64), pl.ds(c * width, width))
        for c in range(PIECES)
    ]

    def upward(i):
        return move(plans[i][0], *plans[i][1], plans[i][3], place - 1, 2 * i)

    def downward(i):
        return move(plans[i][0], *plans[i][2], plans[i][3], place + 1, 2 * i + 1)

    def start_up(*which):
        @pl.when(place > 0)
        def _():
            for i in which:
                upward(i).start()

    def start_down(*which):
        @pl.when(place < n - 1)
        def _():
            for i in which:
                downward(i).start()

    def receive(i):
        @pl.when(place < n - 1)
        def _():
            upward(i).wait_recv()

        @pl.when(place > 0)
        def _():
            downward(i).wait_recv()

    def sent(i):
        @pl.when(place > 0)
        def _():
            upward(i).wait_send()

        @pl.when(place < n - 1)
        def _():
            downward(i).wait_send()

    def narrow(r):
        near[pl.ds(r + edge1, TALL), :] = across(m_ref[pl.ds(r, TALL), :], HALF1, True)

    def finish_first(r):
        y = across(mid[pl.ds(r, TALL), :], HALF1, False)
        first_ref[pl.ds(r, TALL), :] = y
        far[pl.ds(r + edge2, TALL), :] = across(y, HALF2, True)

    row_blocks(0, 64, narrow)
    start_up(0)
    row_blocks(rows - 64, 64, narrow)
    start_down(0)

    @pl.when(is_top)
    def _():
        near[0:edge1, :] = jnp.full((edge1, near.shape[1]), jnp.inf, jnp.float32)
        far[0:edge2, :] = jnp.full((edge2, far.shape[1]), jnp.inf, jnp.float32)

    @pl.when(is_bottom)
    def _():
        near[edge1 + rows :, :] = jnp.full((edge1, near.shape[1]), jnp.inf, jnp.float32)
        far[edge2 + rows :, :] = jnp.full((edge2, far.shape[1]), jnp.inf, jnp.float32)

    row_blocks(64, rows - 128, narrow)
    open_rows(near, edge1, rows - 128, mid, 64, HALF1, None, None)
    row_blocks(64, 64, finish_first)
    start_up(1)
    row_blocks(128, rows - 192, finish_first)
    start_down(1)
    receive(0)
    last = range(2, 2 + PIECES)
    open_rows(near, 0, 64, mid, 0, HALF1, is_top, None)
    row_blocks(0, 64, finish_first)
    start_up(*last)
    open_rows(near, rows - 64, 64, mid, rows - 64, HALF1, None, is_bottom)
    row_blocks(rows - 64, 64, finish_first)
    start_down(*last)
    receive(1)
    tiles = width // BC
    cols = m_ref.shape[1]
    for c in range(PIECES):
        receive(2 + c)
        open_rows(far, 0, rows, mid, 0, HALF2, is_top, is_bottom, c * tiles, (c + 1) * tiles)
        lo = max(c * width - BC, 0)
        hi = (c + 1) * width - BC if c < PIECES - 1 else cols
        left, right = max(lo - BC, 0), min(hi + BC, cols)

        def finish_ground(r, lo=lo, hi=hi, left=left, right=right):
            y = across(mid[pl.ds(r, TALL), left:right], HALF2, False)
            ground_ref[pl.ds(r, TALL), lo:hi] = y[:, lo - left : hi - left]

        row_blocks(0, rows, finish_ground)

    for i in range(2 + PIECES):
        sent(i)


def on_device(n, base_grid, strip_minima, strip_owner, strip_cell):
    held = strip_minima.shape[0]
    capacity = max(2, 2 * held // n)
    rows, cols = base_grid.shape
    vmem = pl.BlockSpec(memory_space=pltpu.VMEM)
    smem = pl.BlockSpec(memory_space=pltpu.SMEM)
    outbox = pl.pallas_call(
        functools.partial(pack_kernel, n, capacity, held),
        out_shape=jax.ShapeDtypeStruct((n, capacity + 1, BR, BC), jnp.float32),
        in_specs=[smem, smem, vmem],
        out_specs=vmem,
        scratch_shapes=[pltpu.SMEM((n,), jnp.int32)],
        compiler_params=pltpu.CompilerParams(vmem_limit_bytes=VMEM_LIMIT),
        name="pack",
    )(strip_owner[:, 0], strip_cell, strip_minima)
    inbox, base = pl.pallas_call(
        functools.partial(exchange_kernel, n),
        out_shape=(
            jax.ShapeDtypeStruct(outbox.shape, jnp.float32),
            jax.ShapeDtypeStruct(base_grid.shape, jnp.float32),
        ),
        in_specs=[vmem, pl.BlockSpec(memory_space=pl.ANY)],
        out_specs=(vmem, vmem),
        scratch_shapes=[
            pltpu.SemaphoreType.DMA((n,)),
            pltpu.SemaphoreType.DMA((n,)),
            pltpu.SemaphoreType.DMA,
            pltpu.SemaphoreType.DMA,
        ],
        compiler_params=pltpu.CompilerParams(
            collective_id=1, has_side_effects=True, vmem_limit_bytes=VMEM_LIMIT
        ),
        name="exchange",
    )(outbox, base_grid)
    tags = inbox[:, capacity, 0, :capacity].astype(jnp.int32).reshape(-1)
    merged = pl.pallas_call(
        functools.partial(merge_kernel, n, capacity, cols // BC),
        out_shape=jax.ShapeDtypeStruct((rows, cols), jnp.float32),
        in_specs=[smem, vmem, vmem],
        out_specs=vmem,
        compiler_params=pltpu.CompilerParams(vmem_limit_bytes=VMEM_LIMIT),
        name="merge",
    )(tags, base, inbox)
    shape = jax.ShapeDtypeStruct((rows, cols), jnp.float32)
    opened_first, ground = pl.pallas_call(
        functools.partial(open_kernel, n),
        out_shape=(shape, shape),
        in_specs=[vmem],
        out_specs=(vmem, vmem),
        scratch_shapes=[
            pltpu.VMEM((rows + 4 * HALF1, cols), jnp.float32),
            pltpu.VMEM((rows + 4 * HALF2, cols), jnp.float32),
            pltpu.VMEM((rows, cols), jnp.float32),
            pltpu.SemaphoreType.DMA((4 + 2 * PIECES,)),
            pltpu.SemaphoreType.DMA((4 + 2 * PIECES,)),
        ],
        compiler_params=pltpu.CompilerParams(
            collective_id=0, has_side_effects=True, vmem_limit_bytes=VMEM_LIMIT
        ),
        name="opening",
    )(merged)
    return (merged, opened_first, ground)


def solution(mesh):
    in_specs = (
        P(("groups", "row"), None),
        P(("groups", "row"), None, None),
        P(("groups", "row"), None),
        P(("groups", "row")),
    )
    out_specs = (P(("groups", "row"), None), P(("groups", "row"), None), P(("groups", "row"), None))
    return jax.shard_map(
        functools.partial(on_device, mesh.shape["row"]),
        mesh=mesh,
        in_specs=in_specs,
        out_specs=out_specs,
        check_vma=False,
    )
```

profile of v0, /device:TPU:12, one launch (start us, length us, event | category | flops | bytes accessed | tf_op | source)
XLA Modules:
  0.0 94.6 jit_solution(8025377716616721777)
XLA Ops:
  0.6 0.0 copy-start
  0.6 1.0 %copy-done = f32[128,8,128]{2,1,0:T(8,128)S(1)} copy-done((f32[128,8,128]{2,1,0:T(8,128)S(1)}, f32[128,8,128]{2,1,0:T(8,128)}, u32[]{:S(2)}) %copy-start) | copy-done | bytes 524312
  1.7 0.0 copy-start.1
  1.7 0.7 copy-done.1
  2.3 0.0 copy-start.2
  2.3 0.7 copy-done.2
  3.0 2.2 %pack.1.box_ref = f32[16,17,8,128]{3,2,1,0:T(8,128)S(1)} custom-call(s32[128]{0:T(128)S(1)} %bitcast.1, s32[128]{0:T(128)S(1)} %copy-done.2, f32[128,8,128]{2,1,0:T(8,128)S(1)} %copy-done), custom_call_target="tpu_custom_call" | custom-call | tf_op jit(solution)/shard_map/pack/pallas_call | solution.py:295
  5.2 28.3 %exchange.1 = (f32[16,17,8,128]{3,2,1,0:T(8,128)S(1)}, f32[256,2048]{1,0:T(8,128)S(1)}) custom-call(f32[16,17,8,128]{3,2,1,0:T(8,128)S(1)} %pack.1.box_ref, f32[256,2048]{1,0:T(8,128)} %grid_ref.1), custom_call_target="tpu_custom_call" | custom-call | tf_op jit(solution)/shard_map/exchange/pallas_call | solution.py:304
  33.5 0.1 convert_element_type.8.tags_ref
  33.6 3.3 %merge.1.m_ref = f32[256,2048]{1,0:T(8,128)} custom-call(s32[256]{0:T(256)S(1)} %convert_element_type.8.tags_ref, f32[256,2048]{1,0:T(8,128)S(1)} %get-tuple-element.8.base_ref, f32[16,17,8,128]{3,2,1,0:T(8,128)S(1)} %get-tuple-element.7.box_ref), custom_call_target="tpu_custom_call" | custom-call | tf_op jit(solution)/shard_map/merge/pallas_call | solution.py:324
  36.9 55.0 %opening.1 = (f32[256,2048]{1,0:T(8,128)S(1)}, f32[256,2048]{1,0:T(8,128)S(1)}) custom-call(f32[256,2048]{1,0:T(8,128)} %merge.1.m_ref), custom_call_target="tpu_custom_call" | custom-call | tf_op jit(solution)/shard_map/opening/pallas_call | solution.py:333
  91.9 1.3 %copy.9 = f32[256,2048]{1,0:T(8,128)} copy(f32[256,2048]{1,0:T(8,128)S(1)} %get-tuple-element.15) | data formatting | bytes 4194304
  93.3 1.3 %copy.10 = f32[256,2048]{1,0:T(8,128)} copy(f32[256,2048]{1,0:T(8,128)S(1)} %get-tuple-element.16) | data formatting | bytes 4194304
  (1 shorter events, 0.0 us)
Async XLA Ops:
  0.6 1.0 %copy-start = (f32[128,8,128]{2,1,0:T(8,128)S(1)}, f32[128,8,128]{2,1,0:T(8,128)}, u32[]{:S(2)}) copy-start(f32[128,8,128]{2,1,0:T(8,128)} %strips_ref.1) | copy-start | bytes 1572868
  1.7 0.7 copy-start.1
  2.3 0.7 copy-start.2
where the time goes:
time: 94.8 us; the launch traced here: 94.6 us
  Pallas kernels  88.8 us (94%)
  local copies, waits for them, and re-layouts  5.06 us (5%)
    pallas_call x1, Pallas kernels, on_device(): pl.pallas_call(functools.partial(open_kernel, n), out_shape=(shape, shape...  55 us
    pallas_call x1, Pallas kernels, on_device(): pl.pallas_call(functools.partial(exchange_kernel, n), out_shape=(jax.Shap...  28.3 us
    unnamed x8, local copies, waits for them, and re-layouts  4.98 us
    pallas_call x1, Pallas kernels, on_device(): pl.pallas_call(functools.partial(merge_kernel, n, capacity, cols // BC),...  3.34 us
    pallas_call x1, Pallas kernels, on_device(): pl.pallas_call(functools.partial(pack_kernel, n, capacity, held), out_sha...  2.2 us

commit v1 on v0

--- a/solution.py
+++ b/solution.py
@@ -276,11 +276,13 @@
         hi = (c + 1) * width - BC if c < PIECES - 1 else cols
         left, right = max(lo - BC, 0), min(hi + BC, cols)
 
-        def finish_ground(r, lo=lo, hi=hi, left=left, right=right):
-            y = across(mid[pl.ds(r, TALL), left:right], HALF2, False)
-            ground_ref[pl.ds(r, TALL), lo:hi] = y[:, lo - left : hi - left]
-
-        row_blocks(0, rows, finish_ground)
+        def finish_ground(i, carry, lo=lo, hi=hi, left=left, right=right):
+            here = pl.ds(pl.multiple_of(i * 2 * TALL, 2 * TALL), 2 * TALL)
+            y = across(mid[here, left:right], HALF2, False)
+            ground_ref[here, lo:hi] = y[:, lo - left : hi - left]
+            return carry
+
+        lax.fori_loop(0, rows // (2 * TALL), finish_ground, 0)
 
     for i in range(2 + PIECES):
         sent(i)

time: 94.8 us -> 91.1 us (0.961)
  the two profiles are of different devices: /device:TPU:12 before, /device:TPU:14 now
where the time goes in v1:
time: 91.1 us; the launch traced here: 91.6 us
  Pallas kernels  85.8 us (94%)
  local copies, waits for them, and re-layouts  5.06 us (6%)
    pallas_call x1, Pallas kernels, on_device(): pl.pallas_call(functools.partial(open_kernel, n), out_shape=(shape, shape...  51.8 us
    pallas_call x1, Pallas kernels, on_device(): pl.pallas_call(functools.partial(exchange_kernel, n), out_shape=(jax.Shap...  28.3 us
    unnamed x8, local copies, waits for them, and re-layouts  4.98 us
    pallas_call x1, Pallas kernels, on_device(): pl.pallas_call(functools.partial(merge_kernel, n, capacity, cols // BC),...  3.51 us
    pallas_call x1, Pallas kernels, on_device(): pl.pallas_call(functools.partial(pack_kernel, n, capacity, held), out_sha...  2.2 us

profile of v1, /device:TPU:14, one launch (start us, length us, event | category | flops | bytes accessed | tf_op | source)
XLA Modules:
  0.0 91.6 jit_solution(3269874301912024465)
XLA Ops:
  0.6 0.0 copy-start
  0.6 1.0 %copy-done = f32[128,8,128]{2,1,0:T(8,128)S(1)} copy-done((f32[128,8,128]{2,1,0:T(8,128)S(1)}, f32[128,8,128]{2,1,0:T(8,128)}, u32[]{:S(2)}) %copy-start) | copy-done | bytes 524312
  1.7 0.0 copy-start.1
  1.7 0.7 copy-done.1
  2.3 0.0 copy-start.2
  2.3 0.7 copy-done.2
  3.0 2.2 %pack.1.box_ref = f32[16,17,8,128]{3,2,1,0:T(8,128)S(1)} custom-call(s32[128]{0:T(128)S(1)} %bitcast.1, s32[128]{0:T(128)S(1)} %copy-done.2, f32[128,8,128]{2,1,0:T(8,128)S(1)} %copy-done), custom_call_target="tpu_custom_call" | custom-call | tf_op jit(solution)/shard_map/pack/pallas_call | solution.py:297
  5.2 28.3 %exchange.1 = (f32[16,17,8,128]{3,2,1,0:T(8,128)S(1)}, f32[256,2048]{1,0:T(8,128)S(1)}) custom-call(f32[16,17,8,128]{3,2,1,0:T(8,128)S(1)} %pack.1.box_ref, f32[256,2048]{1,0:T(8,128)} %grid_ref.1), custom_call_target="tpu_custom_call" | custom-call | tf_op jit(solution)/shard_map/exchange/pallas_call | solution.py:306
  33.5 0.1 convert_element_type.8.tags_ref
  33.6 3.5 %merge.1.m_ref = f32[256,2048]{1,0:T(8,128)} custom-call(s32[256]{0:T(256)S(1)} %convert_element_type.8.tags_ref, f32[256,2048]{1,0:T(8,128)S(1)} %get-tuple-element.8.base_ref, f32[16,17,8,128]{3,2,1,0:T(8,128)S(1)} %get-tuple-element.7.box_ref), custom_call_target="tpu_custom_call" | custom-call | tf_op jit(solution)/shard_map/merge/pallas_call | solution.py:326
  37.1 51.8 %opening.1 = (f32[256,2048]{1,0:T(8,128)S(1)}, f32[256,2048]{1,0:T(8,128)S(1)}) custom-call(f32[256,2048]{1,0:T(8,128)} %merge.1.m_ref), custom_call_target="tpu_custom_call" | custom-call | tf_op jit(solution)/shard_map/opening/pallas_call | solution.py:335
  88.9 1.3 %copy.9 = f32[256,2048]{1,0:T(8,128)} copy(f32[256,2048]{1,0:T(8,128)S(1)} %get-tuple-element.15) | data formatting | bytes 4194304
  90.2 1.3 %copy.10 = f32[256,2048]{1,0:T(8,128)} copy(f32[256,2048]{1,0:T(8,128)S(1)} %get-tuple-element.16) | data formatting | bytes 4194304
  (1 shorter events, 0.0 us)
Async XLA Ops:
  0.6 1.0 %copy-start = (f32[128,8,128]{2,1,0:T(8,128)S(1)}, f32[128,8,128]{2,1,0:T(8,128)}, u32[]{:S(2)}) copy-start(f32[128,8,128]{2,1,0:T(8,128)} %strips_ref.1) | copy-start | bytes 1572868
  1.7 0.7 copy-start.1
  2.3 0.7 copy-start.2
